TPU v7x, 32 devices: a whole 2x2x4 slice. The times are simulated.
32 devices in a mesh: ctx: 2 (over core), head: 16 (over z, y, x).
Axes of the slice: x: 2, y: 2, z: 4, core: 2. Of those that a mesh axis runs over, the one named last changes fastest.
Arguments:
- queries: bfloat16 [32, 24576], P('ctx', 'head'), may hold values from -8 to 8
- cache: bfloat16 [2048, 576], P(('ctx', 'head')), may hold values from -8 to 8
- key_up_weight: bfloat16 [128, 128, 512], P('head', None, 'ctx'), may hold values from -0.5 to 0.5
- value_up_weight: bfloat16 [128, 128, 512], P('head', None, 'ctx'), may hold values from -1.5 to 1.5
- prior_len: int32 [1], replicated, may hold values from 0 to 2016
Outputs:
- attended: bfloat16 [32, 16384], P('ctx', 'head')
All inputs are finite; a program needn't handle non-finite values.
Results may differ from a plain program's by a relative error of at most 0.02.
Values may be sent and summed in bfloat16 or wider, within the bound.
A program may use at most 128 MiB of HBM per device.

v0:
```python
import jax
import jax.numpy as jnp
from jax import lax
from jax.experimental import pallas as pl
from jax.experimental.pallas import tpu as pltpu
from jax.sharding import PartitionSpec as P

PLAIN_WIDTH = 128
ROTARY_WIDTH = 64
LATENT_WIDTH = 512
VALUE_WIDTH = 128


def per_device(queries, cache, key_up_weight, value_up_weight, prior_len):
    heads_number = key_up_weight.shape[0]
    block_rows = queries.shape[0]
    combined_width = LATENT_WIDTH + ROTARY_WIDTH
    key_panel, value_panel = (
        lax.all_gather(key_up_weight, "ctx", axis=2, tiled=True),
        lax.all_gather(value_up_weight, "ctx", axis=2, tiled=True),
    )
    gathered = lax.all_gather(queries, "ctx", axis=0, tiled=True)
    split_rows = gathered.reshape(gathered.shape[0], heads_number, PLAIN_WIDTH + ROTARY_WIDTH)
    latent = jnp.einsum(
        "thn,hnc->thc",
        split_rows[:, :, :PLAIN_WIDTH],
        key_panel,
        preferred_element_type=jnp.float32,
    ).astype(jnp.bfloat16)
    flat_queries = jnp.concatenate([latent, split_rows[:, :, PLAIN_WIDTH:]], axis=2).reshape(
        -1, combined_width
    )
    flat_rows = flat_queries.shape[0]
    query_number = flat_rows // heads_number
    query_place = prior_len[0] + jnp.arange(flat_rows, dtype=jnp.int32) // heads_number
    group_slots = cache.shape[0] * lax.axis_size("head")
    block_base = lax.axis_index("ctx") * group_slots
    score_scale = (PLAIN_WIDTH + ROTARY_WIDTH) ** (-0.5)
    key_section = lax.all_gather(cache, "head", axis=0, tiled=True)
    row_peak = jnp.full((flat_rows,), -1e30, jnp.float32)
    key_count = key_section.shape[0]
    scores = (
        jnp.einsum("rc,nc->rn", flat_queries, key_section, preferred_element_type=jnp.float32)
        * score_scale
    )
    key_place = block_base + jnp.arange(key_count, dtype=jnp.int32)
    visible = key_place[None, :] <= query_place[:, None]
    scores = jnp.where(visible, scores, jnp.float32(-1e30))
    new_peak = jnp.maximum(row_peak, jnp.max(scores, axis=1))
    probabilities = jnp.where(visible, jnp.exp(scores - new_peak[:, None]), jnp.float32(0.0))
    row_total = jnp.sum(probabilities, axis=1)
    weighted_values = jnp.dot(
        probabilities.astype(jnp.bfloat16),
        key_section[:, :LATENT_WIDTH],
        preferred_element_type=jnp.float32,
    )
    row_peak, row_total, weighted_values = (new_peak, row_total, weighted_values)
    global_peak = lax.pmax(row_peak, "ctx")
    softmax_scale = jnp.exp(row_peak - global_peak)
    scaled_sums = (row_total * softmax_scale).reshape(query_number, heads_number)
    latent_scaled = (weighted_values * softmax_scale[:, None]).reshape(
        query_number, heads_number * LATENT_WIDTH
    )
    block_latent, own_totals = (
        lax.psum_scatter(
            latent_scaled.astype(jnp.bfloat16), "ctx", scatter_dimension=0, tiled=True
        ).astype(jnp.float32),
        lax.psum_scatter(
            scaled_sums.astype(jnp.bfloat16), "ctx", scatter_dimension=0, tiled=True
        ).astype(jnp.float32),
    )
    reshaped_queries = block_latent.reshape(block_rows, heads_number, LATENT_WIDTH)
    projected = jnp.einsum(
        "thc,hvc->thv",
        reshaped_queries,
        value_panel.astype(jnp.float32),
        precision=lax.Precision.HIGHEST,
    )
    result = projected / own_totals[:, :, None]
    return result.reshape(block_rows, heads_number * VALUE_WIDTH).astype(jnp.bfloat16)


MESH = pl.DeviceIdType.MESH
HEAD_WIDTH = PLAIN_WIDTH + ROTARY_WIDTH
Z_CHIPS, Y_CHIPS, X_CHIPS = 4, 2, 2
LANES = 128


def fused_kernel(
    queries_hbm, cache_hbm, key_hbm, value_hbm, prior_ref, out_ref,
    queries_ref, cache_ref, mine, key_half, value_panel, query_latent, query_rotary,
    numerator, own_part, peer_part, own_stats, peer_stats,
    mine_recv, half_recv, whole_recv, send_sem, core_recv, local_sem,
):
    core = lax.axis_index("ctx")
    place = lax.axis_index("head")
    z = place // (Y_CHIPS * X_CHIPS)
    y = (place // X_CHIPS) % Y_CHIPS
    x = place % X_CHIPS
    heads = key_hbm.shape[0]
    tokens = queries_hbm.shape[0]
    slots = cache_hbm.shape[0]
    half_slots = slots // 2
    tiles = LATENT_WIDTH // LANES
    half_rows = mine.shape[2] // 2
    core_rows = heads * tokens
    flat_rows = 2 * core_rows

    def chip(zz, yy, xx):
        return (zz * Y_CHIPS + yy) * X_CHIPS + xx

    middle = z % 3 != 0
    levels = [z, 1 + z % 2, 2 - 2 * (z % 2) + z // 2, 3 - 3 * (z // 2)]
    x_peer = (core, chip(z, y, 1 - x))
    y_peer = (core, chip(z, 1 - y, x))
    core_peer = (1 - core, place)
    pair_peer = (core, chip(z + 1 - 2 * (z % 2), y, x))
    mirror_peer = (core, chip(3 - z, y, x))
    partners = [x_peer, y_peer, core_peer, pair_peer, mirror_peer]

    barrier = pltpu.get_barrier_semaphore()
    for partner in partners:
        pl.semaphore_signal(barrier, inc=1, device_id=partner, device_id_type=MESH)

    local = [
        pltpu.make_async_copy(cache_hbm, cache_ref, local_sem.at[0]),
        pltpu.make_async_copy(queries_hbm, queries_ref.at[core], local_sem.at[1]),
        pltpu.make_async_copy(key_hbm, key_half, local_sem.at[2]),
        pltpu.make_async_copy(value_hbm, value_panel.at[core], local_sem.at[3]),
    ]
    for copy in local:
        copy.start()
    local[0].wait()
    for c in range(tiles):
        mine[z, 0, c * slots:(c + 1) * slots, :] = cache_ref[:, c * LANES:(c + 1) * LANES]
    rotary_keys = cache_ref[:, LATENT_WIDTH:]
    mine[z, 0, tiles * slots:, :] = jnp.concatenate(
        [rotary_keys[:half_slots], rotary_keys[half_slots:]], axis=1
    )
    pl.semaphore_wait(barrier, len(partners))

    sends, middle_sends = [], []

    def send(src, dst, recv, to, only_middle=False):
        copy = pltpu.make_async_remote_copy(
            src_ref=src, dst_ref=dst, recv_sem=recv,
            send_sem=send_sem.at[len(sends) + len(middle_sends)],
            device_id=to, device_id_type=MESH,
        )
        if only_middle:
            pl.when(middle)(copy.start)
            middle_sends.append(copy)
        else:
            copy.start()
            sends.append(copy)
        return copy

    def arrived(ref, sem):
        pltpu.make_async_copy(ref, ref, sem).wait()

    def rows(k, p, half):
        return mine.at[k, p, pl.ds(half * half_rows, half_rows)]

    def share_column(k):
        block = mine.at[k, 0]
        send(block, mine.at[k, 1], mine_recv.at[k, 1], x_peer)
        send(block, mine.at[k, 2], mine_recv.at[k, 2], y_peer)

    def along_z(k, to, only_middle):
        return send(mine.at[k, 0], mine.at[k, 0], mine_recv.at[k, 0], to, only_middle)

    def column_step(i):
        k = levels[i]
        arrived(mine.at[k, 0], mine_recv.at[k, 0])
        if i < 3:
            along_z(k, mirror_peer if i == 2 else pair_peer, True)
        share_column(k)

    def plane_step(i):
        k = levels[i]
        arrived(mine.at[k, 1], mine_recv.at[k, 1])
        if i in (0, 3):
            send(rows(k, 1, 1), rows(k, 3, 1), half_recv.at[k, 1], y_peer)
        arrived(mine.at[k, 2], mine_recv.at[k, 2])
        if i in (0, 3):
            send(rows(k, 2, 0), rows(k, 3, 0), half_recv.at[k, 0], x_peer)

    def diagonal_along_z(k, to, only_middle):
        send(mine.at[k, 3], mine.at[k, 3], whole_recv.at[k], to, only_middle)

    def diagonal_step(i):
        k = levels[i]
        if i in (0, 3):
            for half in (0, 1):
                arrived(rows(k, 3, half), half_recv.at[k, half])
        else:
            arrived(mine.at[k, 3], whole_recv.at[k])
        if i == 0:
            diagonal_along_z(k, pair_peer, False)
            diagonal_along_z(k, mirror_peer, True)
        if i == 1:
            diagonal_along_z(k, pair_peer, True)

    def project_queries(first, last):
        zeros = jnp.zeros((2 * tokens, ROTARY_WIDTH), jnp.bfloat16)
        both = jnp.concatenate([queries_ref[0], queries_ref[1]], axis=0)
        for h in range(first, last):
            plain = both[:, h * HEAD_WIDTH:h * HEAD_WIDTH + PLAIN_WIDTH]
            rotary = both[:, h * HEAD_WIDTH + PLAIN_WIDTH:(h + 1) * HEAD_WIDTH]
            latent = jnp.dot(
                plain, key_half[h], preferred_element_type=jnp.float32
            ).astype(jnp.bfloat16)
            low = jnp.concatenate([rotary, zeros], axis=1)
            high = jnp.concatenate([zeros, rotary], axis=1)
            for c in (0, 1):
                there = slice(c * core_rows + h * tokens, c * core_rows + (h + 1) * tokens)
                of = slice(c * tokens, (c + 1) * tokens)
                query_latent[core, there, :] = latent[of]
                query_rotary[0, there, :] = low[of]
                query_rotary[1, there, :] = high[of]

    score_scale = HEAD_WIDTH ** (-0.5)
    group_slots = slots * Z_CHIPS * Y_CHIPS * X_CHIPS

    def attend(state, blocks, part_of=None):
        if part_of is None:
            here = pl.ds(0, flat_rows)
            flat_row = lax.broadcasted_iota(jnp.int32, (flat_rows, 1), 0)
            query_place = prior_ref[0] + flat_row // core_rows * tokens + flat_row % tokens
        else:
            here = pl.ds(pl.multiple_of(part_of * core_rows, core_rows), core_rows)
            flat_row = lax.broadcasted_iota(jnp.int32, (core_rows, 1), 0)
            query_place = prior_ref[0] + part_of * tokens + flat_row % tokens
        blocks = [(levels[i], p) for i, p in blocks]
        bases = []
        for k, p in blocks:
            source = chip(k, 1 - y if p in (2, 3) else y, 1 - x if p in (1, 3) else x)
            bases.append(core * group_slots + source * slots)
        width = 4 * half_slots

        def latent_of(part):
            return jnp.concatenate(
                [
                    jnp.concatenate(
                        [
                            mine[k, p, pl.ds(c * slots + part * half_slots, half_slots), :]
                            for c in range(tiles)
                        ],
                        axis=1,
                    )
                    for k, p in blocks
                ],
                axis=0,
            )

        latents = jnp.concatenate([latent_of(0), latent_of(1)], axis=0)
        rotary = jnp.concatenate(
            [mine[k, p, pl.ds(tiles * slots, half_slots), :] for k, p in blocks], axis=0
        )
        column = lax.broadcasted_iota(jnp.int32, (1, 2 * width), 1)
        key_place = column
        for b in range(8):
            inside = (column >= b * half_slots) & (column < (b + 1) * half_slots)
            shift = bases[b % 4] + (b // 4) * half_slots - b * half_slots
            key_place = key_place + jnp.where(inside, shift, 0)
        contract = (((1,), (1,)), ((), ()))
        rotary_scores = [
            lax.dot_general(
                query_rotary[part, here, :], rotary, contract, preferred_element_type=jnp.float32
            )
            for part in (0, 1)
        ]
        scores = lax.dot_general(
            jnp.concatenate([query_latent[0, here, :], query_latent[1, here, :]], axis=1), latents, contract,
            preferred_element_type=jnp.float32,
        )
        scores = (scores + jnp.concatenate(rotary_scores, axis=1)) * score_scale
        visible = key_place <= query_place
        scores = jnp.where(visible, scores, -1e30)
        peak = jnp.max(scores, axis=1, keepdims=True)
        if state is not None:
            peak = jnp.maximum(peak, state[0])
        probs = jnp.where(visible, jnp.exp(scores - peak), 0.0)
        total = jnp.sum(probs, axis=1, keepdims=True)
        weighted = jnp.dot(
            probs.astype(jnp.bfloat16), latents, preferred_element_type=jnp.float32
        )
        if state is None:
            numerator[here, :] = weighted
        else:
            shrink = jnp.exp(state[0] - peak)
            total = total + state[1] * shrink
            numerator[here, :] = numerator[here, :] * shrink + weighted
        return peak, total

    along_z(z, pair_peer, False)
    own_mirrored = along_z(z, mirror_peer, True)
    share_column(z)
    send(queries_hbm, queries_ref.at[core], core_recv.at[0], core_peer)
    local[1].wait()
    local[2].wait()
    arrived(queries_ref.at[1 - core], core_recv.at[0])
    project_queries(0, heads // 2)
    sends.append(middle_sends.pop(0))
    pl.when(jnp.logical_not(middle))(own_mirrored.start)
    column_step(1)
    plane_step(0)
    project_queries(heads // 2, heads)
    send(query_latent.at[core], query_latent.at[core], core_recv.at[1], core_peer)
    column_step(2)
    send(value_hbm, value_panel.at[core], core_recv.at[2], core_peer)
    diagonal_step(0)
    arrived(query_latent.at[1 - core], core_recv.at[1])
    state = attend(None, [(0, p) for p in range(4)])
    column_step(3)
    diagonal_step(1)
    plane_step(1)
    state = attend(state, [(1, p) for p in range(4)])
    plane_step(2)
    plane_step(3)
    state = attend(state, [(2, 0), (2, 1), (2, 2), (3, 0)])
    diagonal_step(2)
    diagonal_step(3)
    pick = core == 0
    low = [value[:core_rows] for value in state]
    high = [value[core_rows:] for value in state]
    last = [(2, 3), (3, 1), (3, 2), (3, 3)]
    their_state = [jnp.where(pick, b, a) for a, b in zip(low, high)]
    our_state = [jnp.where(pick, a, b) for a, b in zip(low, high)]
    peak, total = attend(their_state, last, 1 - core)
    lane = lax.broadcasted_iota(jnp.int32, (core_rows, LANES), 1)
    own_stats[...] = jnp.where(lane < LANES // 2, peak, total)
    theirs = pl.ds(pl.multiple_of((1 - core) * core_rows, core_rows), core_rows)
    ours = pl.ds(pl.multiple_of(core * core_rows, core_rows), core_rows)
    own_part[...] = numerator[theirs, :].astype(jnp.bfloat16)
    send(own_part, peer_part, core_recv.at[4], core_peer)
    send(own_stats, peer_stats, core_recv.at[3], core_peer)
    our_peak, our_total = attend(our_state, last, core)

    local[3].wait()
    arrived(value_panel.at[1 - core], core_recv.at[2])
    arrived(peer_stats, core_recv.at[3])
    their_peak = peer_stats[:, 0:1]
    their_total = peer_stats[:, LANES // 2:LANES // 2 + 1]
    joint_peak = jnp.maximum(our_peak, their_peak)
    our_weight = jnp.exp(our_peak - joint_peak)
    their_weight = jnp.exp(their_peak - joint_peak)
    joint_total = our_total * our_weight + their_total * their_weight
    our_weight = our_weight / joint_total
    their_weight = their_weight / joint_total
    arrived(peer_part, core_recv.at[4])
    averaged = (
        numerator[ours, :] * our_weight + peer_part[...].astype(jnp.float32) * their_weight
    ).astype(jnp.bfloat16)
    for h in range(heads):
        here = slice(h * tokens, (h + 1) * tokens)
        result = lax.dot_general(
            averaged[here], jnp.concatenate([value_panel[0, h], value_panel[1, h]], axis=1),
            (((1,), (1,)), ((), ())), preferred_element_type=jnp.float32,
        )
        out_ref[:, h * VALUE_WIDTH:(h + 1) * VALUE_WIDTH] = result.astype(jnp.bfloat16)
    for copy in sends:
        copy.wait_send()

    @pl.when(middle)
    def _():
        for copy in middle_sends:
            copy.wait_send()


def per_device_fused(queries, cache, key_up_weight, value_up_weight, prior_len):
    heads = key_up_weight.shape[0]
    tokens = queries.shape[0]
    slots = cache.shape[0]
    block_rows = slots * cache.shape[1] // LANES
    core_rows = heads * tokens
    hbm = pl.BlockSpec(memory_space=pltpu.HBM)
    dma = pltpu.SemaphoreType.DMA
    vmem = pltpu.VMEM
    return pl.pallas_call(
        fused_kernel,
        out_shape=jax.ShapeDtypeStruct((tokens, heads * VALUE_WIDTH), jnp.bfloat16),
        in_specs=[hbm, hbm, hbm, hbm, pl.BlockSpec(memory_space=pltpu.SMEM)],
        out_specs=pl.BlockSpec(memory_space=pltpu.VMEM),
        scratch_shapes=[
            vmem((2,) + queries.shape, jnp.bfloat16),
            vmem(cache.shape, jnp.bfloat16),
            vmem((4, 4, block_rows, LANES), jnp.bfloat16),
            vmem(key_up_weight.shape, jnp.bfloat16),
            vmem((2,) + value_up_weight.shape, jnp.bfloat16),
            vmem((2, 2 * core_rows, LATENT_WIDTH // 2), jnp.bfloat16),
            vmem((2, 2 * core_rows, LANES), jnp.bfloat16),
            vmem((2 * core_rows, LATENT_WIDTH), jnp.float32),
            vmem((core_rows, LATENT_WIDTH), jnp.bfloat16),
            vmem((core_rows, LATENT_WIDTH), jnp.bfloat16),
            vmem((core_rows, LANES), jnp.float32),
            vmem((core_rows, LANES), jnp.float32),
            dma((4, 3)), dma((4, 2)), dma((4,)), dma((32,)), dma((5,)), dma((4,)),
        ],
        compiler_params=pltpu.CompilerParams(
            collective_id=0, has_side_effects=True, vmem_limit_bytes=(64 * 1024 - 10375) * 1024
        ),
    )(queries, cache, key_up_weight, value_up_weight, prior_len)


def solution(mesh):
    in_specs = (
        P("ctx", "head"),
        P(("ctx", "head"), None),
        P("head", None, "ctx"),
        P("head", None, "ctx"),
        P(),
    )
    out_specs = P("ctx", "head")
    chips = Z_CHIPS * Y_CHIPS * X_CHIPS
    body = per_device_fused if mesh.shape["ctx"] == 2 and mesh.shape["head"] == chips else per_device
    return jax.shard_map(
        body, mesh=mesh, in_specs=in_specs, out_specs=out_specs, check_vma=False
    )
```

profile of v0, /device:TPU:1, one launch (start us, length us, event | category | flops | bytes accessed | tf_op | source)
XLA Modules:
  0.0 24.4 jit_solution(13197419062595719757)
XLA Ops:
  0.7 23.1 %shard_map.55 = bf16[16,1024]{1,0:T(8,128)(2,1)S(1)} custom-call(bf16[16,1536]{1,0:T(8,128)(2,1)} %queries_hbm.1, bf16[64,576]{1,0:T(8,128)(2,1)} %cache_hbm.1, bf16[8,128,256]{2,1,0:T(8,128)(2,1)} %key_hbm.1, bf16[8,128,256]{2,1,0:T(8,128)(2,1)} %value_hbm.1, s32[1]{0:T(128)S(6)} %copy.7.prior_ref), custom_call_target="tpu_custom_call" | custom-call | tf_op jit(solution)/shard_map/pallas_call | solution.py:380
  23.8 0.6 %copy.8 = bf16[16,1024]{1,0:T(8,128)(2,1)} copy(bf16[16,1024]{1,0:T(8,128)(2,1)S(1)} %shard_map.55) | data formatting | bytes 65536
where the time goes:
time: 24.5 us; the launch traced here: 24.4 us
  Pallas kernels  23.1 us (94%)
  between operations  0.66 us (3%)
  local copies, waits for them, and re-layouts  0.62 us (3%)
    pallas_call x1, Pallas kernels, per_device_fused(): pl.pallas_call(fused_kernel, out_shape=jax.ShapeDtypeStruct((tokens, head...  23.1 us
    unnamed x1, local copies, waits for them, and re-layouts  0.62 us

commit v1 on v0

--- a/solution.py
+++ b/solution.py
@@ -90,7 +90,7 @@
     queries_hbm, cache_hbm, key_hbm, value_hbm, prior_ref, out_ref,
     queries_ref, cache_ref, mine, key_half, value_panel, query_latent, query_rotary,
     numerator, own_part, peer_part, own_stats, peer_stats,
-    mine_recv, half_recv, whole_recv, send_sem, core_recv, local_sem,
+    mine_recv, rest_recv, half_recv, whole_recv, send_sem, core_recv, local_sem,
 ):
     core = lax.axis_index("ctx")
     place = lax.axis_index("head")
@@ -161,10 +161,16 @@
     def rows(k, p, half):
         return mine.at[k, p, pl.ds(half * half_rows, half_rows)]
 
-    def share_column(k):
-        block = mine.at[k, 0]
-        send(block, mine.at[k, 1], mine_recv.at[k, 1], x_peer)
-        send(block, mine.at[k, 2], mine_recv.at[k, 2], y_peer)
+    def share_column(i):
+        k = levels[i]
+        if i in (0, 3):
+            send(rows(k, 0, 1), rows(k, 1, 1), mine_recv.at[k, 1], x_peer)
+            send(rows(k, 0, 0), rows(k, 2, 0), mine_recv.at[k, 2], y_peer)
+            send(rows(k, 0, 0), rows(k, 1, 0), rest_recv.at[k, 0], x_peer)
+            send(rows(k, 0, 1), rows(k, 2, 1), rest_recv.at[k, 1], y_peer)
+        else:
+            send(mine.at[k, 0], mine.at[k, 1], mine_recv.at[k, 1], x_peer)
+            send(mine.at[k, 0], mine.at[k, 2], mine_recv.at[k, 2], y_peer)
 
     def along_z(k, to, only_middle):
         return send(mine.at[k, 0], mine.at[k, 0], mine_recv.at[k, 0], to, only_middle)
@@ -172,18 +178,25 @@
     def column_step(i):
         k = levels[i]
         arrived(mine.at[k, 0], mine_recv.at[k, 0])
-        if i < 3:
-            along_z(k, mirror_peer if i == 2 else pair_peer, True)
-        share_column(k)
+        if i == 1:
+            along_z(k, pair_peer, True)
+        share_column(i)
 
     def plane_step(i):
         k = levels[i]
-        arrived(mine.at[k, 1], mine_recv.at[k, 1])
         if i in (0, 3):
+            arrived(rows(k, 1, 1), mine_recv.at[k, 1])
             send(rows(k, 1, 1), rows(k, 3, 1), half_recv.at[k, 1], y_peer)
-        arrived(mine.at[k, 2], mine_recv.at[k, 2])
-        if i in (0, 3):
+            arrived(rows(k, 2, 0), mine_recv.at[k, 2])
             send(rows(k, 2, 0), rows(k, 3, 0), half_recv.at[k, 0], x_peer)
+        else:
+            arrived(mine.at[k, 1], mine_recv.at[k, 1])
+            arrived(mine.at[k, 2], mine_recv.at[k, 2])
+
+    def plane_rest(i):
+        k = levels[i]
+        arrived(rows(k, 1, 0), rest_recv.at[k, 0])
+        arrived(rows(k, 2, 1), rest_recv.at[k, 1])
 
     def diagonal_along_z(k, to, only_middle):
         send(mine.at[k, 3], mine.at[k, 3], whole_recv.at[k], to, only_middle)
@@ -295,7 +308,7 @@
 
     along_z(z, pair_peer, False)
     own_mirrored = along_z(z, mirror_peer, True)
-    share_column(z)
+    share_column(0)
     send(queries_hbm, queries_ref.at[core], core_recv.at[0], core_peer)
     local[1].wait()
     local[2].wait()
@@ -305,11 +318,23 @@
     pl.when(jnp.logical_not(middle))(own_mirrored.start)
     column_step(1)
     plane_step(0)
+
+    @pl.when(middle)
+    def _():
+        arrived(mine.at[levels[2], 0], mine_recv.at[levels[2], 0])
+
+    along_z(levels[2], mirror_peer, True)
     project_queries(heads // 2, heads)
     send(query_latent.at[core], query_latent.at[core], core_recv.at[1], core_peer)
-    column_step(2)
+
+    @pl.when(jnp.logical_not(middle))
+    def _():
+        arrived(mine.at[levels[2], 0], mine_recv.at[levels[2], 0])
+
+    share_column(2)
     send(value_hbm, value_panel.at[core], core_recv.at[2], core_peer)
     diagonal_step(0)
+    plane_rest(0)
     arrived(query_latent.at[1 - core], core_recv.at[1])
     state = attend(None, [(0, p) for p in range(4)])
     column_step(3)
@@ -319,6 +344,7 @@
     plane_step(2)
     plane_step(3)
     state = attend(state, [(2, 0), (2, 1), (2, 2), (3, 0)])
+    plane_rest(3)
     diagonal_step(2)
     diagonal_step(3)
     pick = core == 0
@@ -395,7 +421,7 @@
             vmem((core_rows, LATENT_WIDTH), jnp.bfloat16),
             vmem((core_rows, LANES), jnp.float32),
             vmem((core_rows, LANES), jnp.float32),
-            dma((4, 3)), dma((4, 2)), dma((4,)), dma((32,)), dma((5,)), dma((4,)),
+            dma((4, 3)), dma((4, 2)), dma((4, 2)), dma((4,)), dma((40,)), dma((5,)), dma((4,)),
         ],
         compiler_params=pltpu.CompilerParams(
             collective_id=0, has_side_effects=True, vmem_limit_bytes=(64 * 1024 - 10375) * 1024

time: 24.5 us -> 24.6 us (level)
  no operation moved by 1% of the time
where the time goes in v1:
time: 24.6 us; the launch traced here: 24.4 us
  Pallas kernels  23.2 us (94%)
  between operations  0.66 us (3%)
  local copies, waits for them, and re-layouts  0.62 us (3%)
    pallas_call x1, Pallas kernels, per_device_fused(): pl.pallas_call(fused_kernel, out_shape=jax.ShapeDtypeStruct((tokens, head...  23.2 us
    unnamed x1, local copies, waits for them, and re-layouts  0.62 us

profile of v1, /device:TPU:1, one launch (start us, length us, event | category | flops | bytes accessed | tf_op | source)
XLA Modules:
  0.0 24.4 jit_solution(11159555051175088218)
XLA Ops:
  0.7 23.2 %shard_map.55 = bf16[16,1024]{1,0:T(8,128)(2,1)S(1)} custom-call(bf16[16,1536]{1,0:T(8,128)(2,1)} %queries_hbm.1, bf16[64,576]{1,0:T(8,128)(2,1)} %cache_hbm.1, bf16[8,128,256]{2,1,0:T(8,128)(2,1)} %key_hbm.1, bf16[8,128,256]{2,1,0:T(8,128)(2,1)} %value_hbm.1, s32[1]{0:T(128)S(6)} %copy.7.prior_ref), custom_call_target="tpu_custom_call" | custom-call | tf_op jit(solution)/shard_map/pallas_call | solution.py:406
  23.8 0.6 %copy.8 = bf16[16,1024]{1,0:T(8,128)(2,1)} copy(bf16[16,1024]{1,0:T(8,128)(2,1)S(1)} %shard_map.55) | data formatting | bytes 65536

commit v2 on v1

--- a/solution.py
+++ b/solution.py
@@ -84,6 +84,7 @@
 HEAD_WIDTH = PLAIN_WIDTH + ROTARY_WIDTH
 Z_CHIPS, Y_CHIPS, X_CHIPS = 4, 2, 2
 LANES = 128
+LOG2_E = 1.4426950408889634
 
 
 def fused_kernel(
@@ -215,7 +216,6 @@
             diagonal_along_z(k, pair_peer, True)
 
     def project_queries(first, last):
-        zeros = jnp.zeros((2 * tokens, ROTARY_WIDTH), jnp.bfloat16)
         both = jnp.concatenate([queries_ref[0], queries_ref[1]], axis=0)
         for h in range(first, last):
             plain = both[:, h * HEAD_WIDTH:h * HEAD_WIDTH + PLAIN_WIDTH]
@@ -223,16 +223,17 @@
             latent = jnp.dot(
                 plain, key_half[h], preferred_element_type=jnp.float32
             ).astype(jnp.bfloat16)
-            low = jnp.concatenate([rotary, zeros], axis=1)
-            high = jnp.concatenate([zeros, rotary], axis=1)
+            twice = jnp.concatenate([rotary, rotary], axis=1)
             for c in (0, 1):
                 there = slice(c * core_rows + h * tokens, c * core_rows + (h + 1) * tokens)
                 of = slice(c * tokens, (c + 1) * tokens)
                 query_latent[core, there, :] = latent[of]
-                query_rotary[0, there, :] = low[of]
-                query_rotary[1, there, :] = high[of]
-
-    score_scale = HEAD_WIDTH ** (-0.5)
+                query_rotary[there, :] = twice[of]
+
+    score_scale = HEAD_WIDTH ** (-0.5) * LOG2_E
+    key_lane = lax.broadcasted_iota(jnp.int32, (1, LANES), 1)
+    low_lanes = jnp.where(key_lane < ROTARY_WIDTH, 1.0, 0.0).astype(jnp.bfloat16)
+    high_lanes = jnp.where(key_lane < ROTARY_WIDTH, 0.0, 1.0).astype(jnp.bfloat16)
     group_slots = slots * Z_CHIPS * Y_CHIPS * X_CHIPS
 
     def attend(state, blocks, part_of=None):
@@ -276,24 +277,20 @@
             inside = (column >= b * half_slots) & (column < (b + 1) * half_slots)
             shift = bases[b % 4] + (b // 4) * half_slots - b * half_slots
             key_place = key_place + jnp.where(inside, shift, 0)
-        contract = (((1,), (1,)), ((), ()))
-        rotary_scores = [
-            lax.dot_general(
-                query_rotary[part, here, :], rotary, contract, preferred_element_type=jnp.float32
-            )
-            for part in (0, 1)
-        ]
+        keys = jnp.concatenate(
+            [latents, jnp.concatenate([rotary * low_lanes, rotary * high_lanes], axis=0)], axis=1
+        )
+        query = jnp.concatenate(
+            [query_latent[0, here, :], query_latent[1, here, :], query_rotary[here, :]], axis=1
+        )
         scores = lax.dot_general(
-            jnp.concatenate([query_latent[0, here, :], query_latent[1, here, :]], axis=1), latents, contract,
-            preferred_element_type=jnp.float32,
-        )
-        scores = (scores + jnp.concatenate(rotary_scores, axis=1)) * score_scale
-        visible = key_place <= query_place
-        scores = jnp.where(visible, scores, -1e30)
-        peak = jnp.max(scores, axis=1, keepdims=True)
+            query, keys, (((1,), (1,)), ((), ())), preferred_element_type=jnp.float32
+        )
+        scores = jnp.where(key_place <= query_place, scores * score_scale, -1e30)
+        peak = jnp.maximum(jnp.max(scores, axis=1, keepdims=True), -1e29)
         if state is not None:
             peak = jnp.maximum(peak, state[0])
-        probs = jnp.where(visible, jnp.exp(scores - peak), 0.0)
+        probs = jnp.exp2(scores - peak)
         total = jnp.sum(probs, axis=1, keepdims=True)
         weighted = jnp.dot(
             probs.astype(jnp.bfloat16), latents, preferred_element_type=jnp.float32
@@ -301,7 +298,7 @@
         if state is None:
             numerator[here, :] = weighted
         else:
-            shrink = jnp.exp(state[0] - peak)
+            shrink = jnp.exp2(state[0] - peak)
             total = total + state[1] * shrink
             numerator[here, :] = numerator[here, :] * shrink + weighted
         return peak, total
@@ -369,8 +366,8 @@
     their_peak = peer_stats[:, 0:1]
     their_total = peer_stats[:, LANES // 2:LANES // 2 + 1]
     joint_peak = jnp.maximum(our_peak, their_peak)
-    our_weight = jnp.exp(our_peak - joint_peak)
-    their_weight = jnp.exp(their_peak - joint_peak)
+    our_weight = jnp.exp2(our_peak - joint_peak)
+    their_weight = jnp.exp2(their_peak - joint_peak)
     joint_total = our_total * our_weight + their_total * their_weight
     our_weight = our_weight / joint_total
     their_weight = their_weight / joint_total
@@ -415,7 +412,7 @@
             vmem(key_up_weight.shape, jnp.bfloat16),
             vmem((2,) + value_up_weight.shape, jnp.bfloat16),
             vmem((2, 2 * core_rows, LATENT_WIDTH // 2), jnp.bfloat16),
-            vmem((2, 2 * core_rows, LANES), jnp.bfloat16),
+            vmem((2 * core_rows, LANES), jnp.bfloat16),
             vmem((2 * core_rows, LATENT_WIDTH), jnp.float32),
             vmem((core_rows, LATENT_WIDTH), jnp.bfloat16),
             vmem((core_rows, LATENT_WIDTH), jnp.bfloat16),

time: 24.6 us -> 24.7 us (level)
  no operation moved by 1% of the time
where the time goes in v2:
time: 24.7 us; the launch traced here: 24.6 us
  Pallas kernels  23.3 us (94%)
  between operations  0.66 us (3%)
  local copies, waits for them, and re-layouts  0.62 us (3%)
    pallas_call x1, Pallas kernels, per_device_fused(): pl.pallas_call(fused_kernel, out_shape=jax.ShapeDtypeStruct((tokens, head...  23.3 us
    unnamed x1, local copies, waits for them, and re-layouts  0.62 us

profile of v2, /device:TPU:1, one launch (start us, length us, event | category | flops | bytes accessed | tf_op | source)
XLA Modules:
  0.0 24.6 jit_solution(17510853616432241785)
XLA Ops:
  0.7 23.3 %shard_map.55 = bf16[16,1024]{1,0:T(8,128)(2,1)S(1)} custom-call(bf16[16,1536]{1,0:T(8,128)(2,1)} %queries_hbm.1, bf16[64,576]{1,0:T(8,128)(2,1)} %cache_hbm.1, bf16[8,128,256]{2,1,0:T(8,128)(2,1)} %key_hbm.1, bf16[8,128,256]{2,1,0:T(8,128)(2,1)} %value_hbm.1, s32[1]{0:T(128)S(6)} %copy.7.prior_ref), custom_call_target="tpu_custom_call" | custom-call | tf_op jit(solution)/shard_map/pallas_call | solution.py:403
  24.0 0.6 %copy.8 = bf16[16,1024]{1,0:T(8,128)(2,1)} copy(bf16[16,1024]{1,0:T(8,128)(2,1)S(1)} %shard_map.55) | data formatting | bytes 65536

commit v3 on v1

--- a/solution.py
+++ b/solution.py
@@ -249,7 +249,8 @@
         for k, p in blocks:
             source = chip(k, 1 - y if p in (2, 3) else y, 1 - x if p in (1, 3) else x)
             bases.append(core * group_slots + source * slots)
-        width = 4 * half_slots
+        count = len(blocks)
+        width = count * half_slots
 
         def latent_of(part):
             return jnp.concatenate(
@@ -272,9 +273,9 @@
         )
         column = lax.broadcasted_iota(jnp.int32, (1, 2 * width), 1)
         key_place = column
-        for b in range(8):
+        for b in range(2 * count):
             inside = (column >= b * half_slots) & (column < (b + 1) * half_slots)
-            shift = bases[b % 4] + (b // 4) * half_slots - b * half_slots
+            shift = bases[b % count] + (b // count) * half_slots - b * half_slots
             key_place = key_place + jnp.where(inside, shift, 0)
         contract = (((1,), (1,)), ((), ()))
         rotary_scores = [
@@ -336,11 +337,10 @@
     diagonal_step(0)
     plane_rest(0)
     arrived(query_latent.at[1 - core], core_recv.at[1])
-    state = attend(None, [(0, p) for p in range(4)])
     column_step(3)
     diagonal_step(1)
     plane_step(1)
-    state = attend(state, [(1, p) for p in range(4)])
+    state = attend(None, [(i, p) for i in (0, 1) for p in range(4)])
     plane_step(2)
     plane_step(3)
     state = attend(state, [(2, 0), (2, 1), (2, 2), (3, 0)])

time: 24.6 us -> 24.6 us (level)
  no operation moved by 1% of the time
where the time goes in v3:
time: 24.6 us; the launch traced here: 24.4 us
  Pallas kernels  23.2 us (94%)
  between operations  0.66 us (3%)
  local copies, waits for them, and re-layouts  0.62 us (3%)
    pallas_call x1, Pallas kernels, per_device_fused(): pl.pallas_call(fused_kernel, out_shape=jax.ShapeDtypeStruct((tokens, head...  23.2 us
    unnamed x1, local copies, waits for them, and re-layouts  0.62 us

profile of v3, /device:TPU:1, one launch (start us, length us, event | category | flops | bytes accessed | tf_op | source)
XLA Modules:
  0.0 24.4 jit_solution(16907874081696452703)
XLA Ops:
  0.7 23.2 %shard_map.55 = bf16[16,1024]{1,0:T(8,128)(2,1)S(1)} custom-call(bf16[16,1536]{1,0:T(8,128)(2,1)} %queries_hbm.1, bf16[64,576]{1,0:T(8,128)(2,1)} %cache_hbm.1, bf16[8,128,256]{2,1,0:T(8,128)(2,1)} %key_hbm.1, bf16[8,128,256]{2,1,0:T(8,128)(2,1)} %value_hbm.1, s32[1]{0:T(128)S(6)} %copy.7.prior_ref), custom_call_target="tpu_custom_call" | custom-call | tf_op jit(solution)/shard_map/pallas_call | solution.py:406
  23.8 0.6 %copy.8 = bf16[16,1024]{1,0:T(8,128)(2,1)} copy(bf16[16,1024]{1,0:T(8,128)(2,1)S(1)} %shard_map.55) | data formatting | bytes 65536
